TPU v7x, 32 devices: a whole 2x2x4 slice. The times are simulated.
32 devices in a mesh: section: 4 (over z), sector: 4 (over y, core), comp: 2 (over x).
Axes of the slice: x: 2, y: 2, z: 4, core: 2. Of those that a mesh axis runs over, the one named last changes fastest.
Arguments:
- env_in: bfloat16 [2, 8, 4, 512, 128], P('comp', None, 'sector', 'section'), may hold values from -6 to 6
- site_tensor: bfloat16 [3, 4, 512, 4, 512], P(None, 'sector', None, None, 'section'), may hold values from -0.125 to 0.125
- bra_tensor: bfloat16 [3, 4, 128, 4, 128], P(None, 'sector'), may hold values from -0.5 to 0.5
- mixing: float32 [3, 4, 8, 8], replicated, may hold values from -2 to 2
- sector_sizes: int32 [4, 4], replicated, may hold values from 256 to 512, as said below
- targets: int32 [3, 4, 4], replicated, may hold values from 0 to 3, as said below
Outputs:
- env_out: bfloat16 [3, 2, 8, 4, 512, 128], P(None, 'comp', None, 'sector', 'section')
- total_env: bfloat16 [8, 4, 512, 128], P('comp', 'sector', 'section')
Inputs may be any that keep to these rules, and one draw needn't show every extreme that they name: `sector_sizes`: on every bond some sector has exactly 512 states. For each site and source sector a the 4 targets are distinct and differ from a by at most 3; at every site some target lies 3 above its source sector and some 3 below.
All inputs are finite; a program needn't handle non-finite values.
Results may differ from a plain program's by a relative error of at most 0.02.
Values may be sent and summed in bfloat16 or wider, within the bound.
A program may use at most 64 MiB of HBM per device.

v0:
```python
import jax
import jax.numpy as jnp
from jax import lax
from jax.sharding import PartitionSpec as P


def local(env_in, site_tensor, bra_tensor, mixing, sector_sizes, targets):
    section_index = lax.axis_index("section")
    sector_index = lax.axis_index("sector")
    sector_count = lax.axis_size("sector")
    site_count = site_tensor.shape[0]
    full_rows = site_tensor.shape[2]
    local_rows = site_tensor.shape[4]
    row_ids = jnp.arange(full_rows, dtype=jnp.int32)
    own_rows = section_index * local_rows + jnp.arange(local_rows, dtype=jnp.int32)
    keep_first = (own_rows < sector_sizes[0, sector_index]).astype(jnp.bfloat16)
    current = env_in[:, :, 0] * keep_first[None, None, :, None]
    results = []
    for site_index in range(site_count):
        targets_row = targets[site_index, sector_index]
        size_out = sector_sizes[site_index + 1][targets_row]
        keep_in = (row_ids < sector_sizes[site_index, sector_index]).astype(jnp.bfloat16)
        keep_out = (own_rows[None, :] < size_out[:, None]).astype(jnp.bfloat16)
        masked = site_tensor[site_index, 0] * keep_in[:, None, None] * keep_out[None, :, :]
        weights = mixing[site_index]
        mixed_rows = jnp.einsum(
            "sdc,bcik->bdsik",
            weights,
            lax.all_gather(current, "section", axis=2, tiled=True).astype(jnp.float32),
            precision=lax.Precision.HIGHEST,
        ).astype(jnp.bfloat16)
        left_total = jnp.einsum(
            "iso,bdsik->bdsok", masked, mixed_rows, preferred_element_type=jnp.float32
        )
        left_part = left_total.astype(jnp.bfloat16)
        partial_value = jnp.einsum(
            "bdsok,ksl->bdsol",
            left_part,
            bra_tensor[site_index, 0],
            preferred_element_type=jnp.float32,
        ).astype(jnp.bfloat16)
        onehot = (
            targets_row[None, :] == jnp.arange(sector_count, dtype=jnp.int32)[:, None]
        ).astype(jnp.bfloat16)
        outgoing = jnp.einsum(
            "js,bdsol->jbdol", onehot, partial_value, preferred_element_type=jnp.float32
        ).astype(jnp.bfloat16)
        received = lax.all_to_all(outgoing, "sector", split_axis=0, concat_axis=0, tiled=True)
        updated = jnp.sum(received, axis=0, dtype=jnp.float32)
        current = updated.astype(jnp.bfloat16)
        results.append(current)
    stacked = jnp.stack(results)[:, :, :, None]
    batch_term = jnp.sum(current.astype(jnp.float32), axis=0)
    summed = lax.psum_scatter(
        batch_term.astype(jnp.bfloat16), "comp", scatter_dimension=0, tiled=True
    )
    return (stacked, summed[:, None])


def solution(mesh):
    in_specs = (
        P("comp", None, "sector", "section", None),
        P(None, "sector", None, None, "section"),
        P(None, "sector", None, None, None),
        P(),
        P(),
        P(),
    )
    out_specs = (
        P(None, "comp", None, "sector", "section", None),
        P("comp", "sector", "section", None),
    )
    return jax.shard_map(local, mesh=mesh, in_specs=in_specs, out_specs=out_specs, check_vma=False)
```

profile of v0, /device:TPU:0, one launch (start us, length us, event | category | flops | bytes accessed | tf_op | source)
XLA Modules:
  0.0 202.3 jit_solution(12540820073185199314)
XLA Ops:
  7.2 1.5 constant_dynamic-slice_fusion.4
  9.3 1.9 bitcast_multiply_fusion.3
  11.3 0.8 slice_bitcast_fusion
  12.1 0.7 fusion.74
  12.8 0.6 gather_fusion.1
  13.4 0.6 gather_fusion.2
  14.1 0.6 gather_fusion
  14.7 0.6 fusion.62
  15.4 0.7 fusion.77
  16.1 1.3 fusion.65
  17.5 1.2 fusion.78
  18.6 2.8 %fusion.45 = (bf16[512,4,128,1]{2,1,0,3:T(4,128)(2,1)S(1)}, bf16[512,4,128,1]{2,1,0,3:T(4,128)(2,1)S(1)}, bf16[512,4,128,1]{2,1,0,3:T(4,128)(2,1)S(1)}) fusion(bf16[3,1,512,4,128]{4,3,2,1,0:T(4,128)(2,1)S(1)} %copy-done, bf16[512]{0:T(512)(128)(2,1)S(1)} %get-tuple-element.32, bf16[4,128]{1,0:T(4,128)(2,1)S(1)} %get-tuple-element.26, ...), kind=kLoop, calls=%fused_computation.40 | loop fusion | flops 1572864 | bytes 3151872 | tf_op jit(solution)/shard_map/mul | solution.py:24
  21.5 20.5 %all-gather.6.cloned.1.call-done = bf16[1,8,512,128]{3,1,0,2:T(8,128)(2,1)} async-done(((bf16[1,8,128,128]{3,1,0,2:T(8,128)(2,1)}), bf16[1,8,512,128]{3,1,0,2:T(8,128)(2,1)}) %all-gather.6.cloned.1.call-update) | async-done | bytes 1048592 | tf_op jit(solution)/shard_map/all_gather | solution.py:29
  42.0 6.6 %convert_bitcast_fusion.2 = bf16[8,4,512,128]{3,0,1,2:T(8,128)(2,1)} fusion(bf16[1,8,512,128]{3,1,0,2:T(8,128)(2,1)} %all-gather.6.cloned.1.call-done, f32[3,4,8,8]{3,2,1,0:T(8,128)} %param.9), kind=kOutput, calls=%fused_computation.11 | convolution fusion | flops 203423744 | bytes 5259264 | tf_op jit(solution)/shard_map/sdc,bcik->bdsik/dot_general | solution.py:26
  48.6 4.4 %fusion.15 = bf16[8,4,128,128]{3,2,0,1:T(8,128)(2,1)S(1)} fusion(bf16[8,4,512,128]{3,0,1,2:T(8,128)(2,1)} %convert_bitcast_fusion.2, bf16[512,4,128,1]{2,1,0,3:T(4,128)(2,1)S(1)} %get-tuple-element.9, bf16[1,1,128,4,128]{4,3,2,1,0:T(4,128)(2,1)S(1)} %get-tuple-element.13), kind=kOutput, calls=%fused_computation.21 | convolution fusion | flops 672137216 | bytes 5898240 | tf_op jit(solution)/shard_map/bdsok,ksl->bdsol/dot_general | solution.py:36
  53.0 0.9 fusion.16
  54.2 17.0 %all_to_all.15 = bf16[4,1,8,128,128]{4,3,2,1,0:T(8,128)(2,1)S(1)} all-to-all(bf16[4,1,8,128,128]{4,3,2,1,0:T(8,128)(2,1)S(1)} %copy.50), channel_id=1, replica_groups=mesh['section'=4,'sector'=4,'comp'=2] {'sector'}, dimensions={0} | all-to-all | bytes 2097152 | tf_op jit(solution)/shard_map/all_to_all | solution.py:48
  71.4 0.9 copy.52
  72.5 26.4 %all-gather.8.cloned.1.call-done = bf16[8,512,128]{2,0,1:T(8,128)(2,1)} async-done(((bf16[8,128,128]{2,0,1:T(8,128)(2,1)}), bf16[8,512,128]{2,0,1:T(8,128)(2,1)}) %all-gather.8.cloned.1.call-update) | async-done | bytes 1048592 | tf_op jit(solution)/shard_map/all_gather | solution.py:29
  99.0 6.2 %convert_bitcast_fusion.1 = bf16[8,4,512,128]{3,0,1,2:T(8,128)(2,1)} fusion(bf16[8,512,128]{2,0,1:T(8,128)(2,1)} %all-gather.8.cloned.1.call-done, f32[3,4,8,8]{3,2,1,0:T(8,128)S(1)} %copy-done.1), kind=kOutput, calls=%fused_computation.10 | convolution fusion | flops 203423744 | bytes 5259264 | tf_op jit(solution)/shard_map/sdc,bcik->bdsik/dot_general | solution.py:26
  105.2 4.4 %fusion.17 = bf16[8,4,128,128]{3,2,0,1:T(8,128)(2,1)S(1)} fusion(bf16[8,4,512,128]{3,0,1,2:T(8,128)(2,1)} %convert_bitcast_fusion.1, bf16[512,4,128,1]{2,1,0,3:T(4,128)(2,1)S(1)} %get-tuple-element.10, bf16[1,1,128,4,128]{4,3,2,1,0:T(4,128)(2,1)S(1)} %get-tuple-element.12), kind=kOutput, calls=%fused_computation.23 | convolution fusion | flops 672137216 | bytes 5898240 | tf_op jit(solution)/shard_map/bdsok,ksl->bdsol/dot_general | solution.py:36
  109.6 0.9 fusion.18
  110.8 17.0 %all_to_all.16 = bf16[4,1,8,128,128]{4,3,2,1,0:T(8,128)(2,1)S(1)} all-to-all(bf16[4,1,8,128,128]{4,3,2,1,0:T(8,128)(2,1)S(1)} %copy.58), channel_id=1, replica_groups=mesh['section'=4,'sector'=4,'comp'=2] {'sector'}, dimensions={0} | all-to-all | bytes 2097152 | tf_op jit(solution)/shard_map/all_to_all | solution.py:48
  128.0 0.9 copy.60
  129.0 26.6 %all-gather.10.cloned.1.call-done = bf16[8,512,128]{2,0,1:T(8,128)(2,1)} async-done(((bf16[8,128,128]{2,0,1:T(8,128)(2,1)}), bf16[8,512,128]{2,0,1:T(8,128)(2,1)}) %all-gather.10.cloned.1.call-update) | async-done | bytes 1048592 | tf_op jit(solution)/shard_map/all_gather | solution.py:29
  155.6 6.2 %convert_bitcast_fusion = bf16[8,4,512,128]{3,0,1,2:T(8,128)(2,1)} fusion(bf16[8,512,128]{2,0,1:T(8,128)(2,1)} %all-gather.10.cloned.1.call-done, f32[3,4,8,8]{3,2,1,0:T(8,128)S(1)} %copy-done.1), kind=kOutput, calls=%fused_computation.9 | convolution fusion | flops 203423744 | bytes 5259264 | tf_op jit(solution)/shard_map/sdc,bcik->bdsik/dot_general | solution.py:26
  161.8 4.4 %fusion.19 = bf16[8,4,128,128]{3,2,0,1:T(8,128)(2,1)S(1)} fusion(bf16[8,4,512,128]{3,0,1,2:T(8,128)(2,1)} %convert_bitcast_fusion, bf16[512,4,128,1]{2,1,0,3:T(4,128)(2,1)S(1)} %get-tuple-element.8, bf16[1,1,128,4,128]{4,3,2,1,0:T(4,128)(2,1)S(1)} %get-tuple-element.11), kind=kOutput, calls=%fused_computation.25 | convolution fusion | flops 672137216 | bytes 5898240 | tf_op jit(solution)/shard_map/bdsok,ksl->bdsol/dot_general | solution.py:36
  166.2 0.9 fusion.20
  167.4 17.0 %all_to_all.17 = bf16[4,1,8,128,128]{4,3,2,1,0:T(8,128)(2,1)S(1)} all-to-all(bf16[4,1,8,128,128]{4,3,2,1,0:T(8,128)(2,1)S(1)} %copy.66), channel_id=1, replica_groups=mesh['section'=4,'sector'=4,'comp'=2] {'sector'}, dimensions={0} | all-to-all | bytes 2097152 | tf_op jit(solution)/shard_map/all_to_all | solution.py:48
  184.4 0.9 reduce_sum.48
  185.3 1.9 maximum_bitcast_fusion
  187.3 8.5 %reduce-scatter.2.cloned.1.call-done = bf16[4,128,128]{2,1,0:T(8,128)(2,1)} async-done(((bf16[8,128,128]{2,1,0:T(8,128)(2,1)}), bf16[4,128,128]{2,1,0:T(8,128)(2,1)}) %reduce-scatter.2.cloned.1.call-update) | async-done | bytes 131088 | tf_op jit(solution)/shard_map/reduce_scatter | solution.py:54
  (22 shorter events, 2.3 us)
Async XLA Ops:
  7.2 11.5 %copy-start = (bf16[3,1,512,4,128]{4,3,2,1,0:T(4,128)(2,1)S(1)}, bf16[3,1,512,4,128]{4,3,2,1,0:T(4,128)(2,1)}, u32[]{:S(2)}) copy-start(bf16[3,1,512,4,128]{4,3,2,1,0:T(4,128)(2,1)} %param.7) | copy-start | bytes 4718596
  7.2 34.8 %all-gather.6.cloned.1.call-start = ((), (), s32[]{:S(2)}) async-start(), calls=%async_computation.4 | async-start | bytes 1310720 | tf_op jit(solution)/shard_map/all_gather | solution.py:29
  11.2 87.8 %all-gather.8.cloned.1.call-start = ((), (), s32[]{:S(2)}) async-start(), calls=%async_computation.6 | async-start | bytes 1310720 | tf_op jit(solution)/shard_map/all_gather | solution.py:29
  53.0 46.0 %copy-start.1 = (f32[3,4,8,8]{3,2,1,0:T(8,128)S(1)}, f32[3,4,8,8]{3,2,1,0:T(8,128)}, u32[]{:S(2)}) copy-start(f32[3,4,8,8]{3,2,1,0:T(8,128)} %param.9) | copy-start | bytes 9220
  72.3 83.3 %all-gather.10.cloned.1.call-start = ((), (), s32[]{:S(2)}) async-start(), calls=%async_computation.7 | async-start | bytes 1310720 | tf_op jit(solution)/shard_map/all_gather | solution.py:29
  128.9 66.8 %reduce-scatter.2.cloned.1.call-start = ((), (), s32[]{:S(2)}) async-start(), calls=%async_computation.5 | async-start | bytes 393216 | tf_op jit(solution)/shard_map/reduce_scatter | solution.py:54
Sparse Core Ops, SparseCore 0:
  11.3 30.6 all-gather.5
  72.4 26.5 all-gather.7
  129.0 26.5 all-gather.9
  185.5 10.2 reduce-scatter.1
where the time goes:
time: 203 us; the launch traced here: 202 us
  waiting for transfers between devices  82.1 us (40%)
  blocking collectives  51 us (25%)
  matrix products  35 us (17%)
  between operations  13.9 us (7%)
  other arithmetic  11.3 us (6%)
  local copies, waits for them, and re-layouts  8.57 us (4%)
    all_gather x3, waiting for transfers between devices, local(): lax.all_gather(current, 'section', axis=2, tiled=True).astype(jnp.float32)  73.6 us
    all_to_all x3, blocking collectives, local(): lax.all_to_all(outgoing, 'sector', split_axis=0, concat_axis=0, tiled=True)  51 us
    dot_general x3, matrix products, local(): jnp.einsum('sdc,bcik->bdsik', weights, lax.all_gather(current, 'section',...  19.1 us
    dot_general x3, matrix products, local(): jnp.einsum('bdsok,ksl->bdsol', left_part, bra_tensor[site_index, 0], pref...  13.2 us
    reduce_scatter x1, waiting for transfers between devices, local(): lax.psum_scatter(batch_term.astype(jnp.bfloat16), 'comp', scatter_dimensi...  8.49 us
  transfers between devices with their start and end apart: 4, of which 4 were waited for; matrix products, arithmetic and copies ran while one was open for 6% of the time, Pallas kernels for 0%

commit v1 on v0

--- a/solution.py
+++ b/solution.py
@@ -2,6 +2,22 @@
 import jax.numpy as jnp
 from jax import lax
 from jax.sharding import PartitionSpec as P
+
+
+def gather_around(x, axis, dim):
+    ways, here, lap = (lax.axis_size(axis), lax.axis_index(axis), x.shape[dim])
+    lengths = [n * ways if d == dim else n for d, n in enumerate(x.shape)]
+    full = lax.dynamic_update_slice_in_dim(jnp.zeros(lengths, x.dtype), x, here * lap, axis=dim)
+    going_up = going_down = x
+    for far in range(1, ways // 2 + 1):
+        going_up = lax.ppermute(going_up, axis, [(d, (d + 1) % ways) for d in range(ways)])
+        full = lax.dynamic_update_slice_in_dim(full, going_up, (here - far) % ways * lap, axis=dim)
+        if 2 * far < ways:
+            going_down = lax.ppermute(going_down, axis, [(d, (d - 1) % ways) for d in range(ways)])
+            full = lax.dynamic_update_slice_in_dim(
+                full, going_down, (here + far) % ways * lap, axis=dim
+            )
+    return full
 
 
 def local(env_in, site_tensor, bra_tensor, mixing, sector_sizes, targets):
@@ -26,7 +42,7 @@
         mixed_rows = jnp.einsum(
             "sdc,bcik->bdsik",
             weights,
-            lax.all_gather(current, "section", axis=2, tiled=True).astype(jnp.float32),
+            gather_around(current, "section", 2).astype(jnp.float32),
             precision=lax.Precision.HIGHEST,
         ).astype(jnp.bfloat16)
         left_total = jnp.einsum(

time: 203 us -> 181 us (0.89)
  waiting for transfers between devices: 82.1 us -> 47 us
  starting transfers between devices: 0.34 us -> 12.9 us
  matrix products: 35 us -> 31.3 us
  local copies, waits for them, and re-layouts: 8.57 us -> 12.1 us
    all_gather x3 -> x0, waiting for transfers between devices: 73.6 us -> none  [local(): lax.all_gather(current, 'section', axis=2, tiled=True).astype(jnp.float32)]
    ppermute x0 -> x9, waiting for transfers between devices: none -> 39.9 us  [the longest x6 35.6 us: gather_around(): lax.ppermute(going_up, axis, [(d, (d + 1) % ways) for d in range(ways)])]
    ppermute x0 -> x9, starting transfers between devices: none -> 12.8 us  [the longest x3 9.65 us: gather_around(): lax.ppermute(going_down, axis, [(d, (d - 1) % ways) for d in range(ways)])]
    dynamic_update_slice x0 -> x12, local copies, waits for them, and re-layouts: none -> 4.19 us  [the longest x6 2.1 us: gather_around(): lax.dynamic_update_slice_in_dim(full, going_up, (here - far) % ways * lap...]
    dot_general x3, matrix products: 19.1 us -> 15.4 us  [local(): jnp.einsum('sdc,bcik->bdsik', weights, gather_around(current, 'section',...]
  transfers between devices with their start and end apart: 4 -> 10, of which waited for: 4 -> 8; matrix products, arithmetic and copies ran while one was open for 6% -> 10% of each run, Pallas kernels for 0% -> 0%
where the time goes in v1:
time: 181 us
  blocking collectives  50.8 us (28%)
  waiting for transfers between devices  47 us (26%)
  matrix products  31.3 us (17%)
  between operations  14.3 us (8%)
  starting transfers between devices  12.9 us (7%)
  other arithmetic  12.2 us (7%)
  local copies, waits for them, and re-layouts  12.1 us (7%)
    all_to_all x3, blocking collectives, local(): lax.all_to_all(outgoing, 'sector', split_axis=0, concat_axis=0, tiled=True)  50.8 us
    ppermute x6, waiting for transfers between devices, gather_around(): lax.ppermute(going_up, axis, [(d, (d + 1) % ways) for d in range(ways)])  35.6 us
    dot_general x3, matrix products, local(): jnp.einsum('sdc,bcik->bdsik', weights, gather_around(current, 'section',...  15.4 us
    dot_general x3, matrix products, local(): jnp.einsum('bdsok,ksl->bdsol', left_part, bra_tensor[site_index, 0], pref...  13.2 us
    ppermute x3, starting transfers between devices, gather_around(): lax.ppermute(going_down, axis, [(d, (d - 1) % ways) for d in range(ways)])  9.65 us
    reduce_scatter x1, waiting for transfers between devices, local(): lax.psum_scatter(batch_term.astype(jnp.bfloat16), 'comp', scatter_dimensi...  7.15 us
    ppermute x3, waiting for transfers between devices, gather_around(): lax.ppermute(going_down, axis, [(d, (d - 1) % ways) for d in range(ways)])  4.25 us
  transfers between devices with their start and end apart: 10, of which 8 were waited for; matrix products, arithmetic and copies ran while one was open for 10% of the time, Pallas kernels for 0%

profile of v1, /device:TPU:0, one launch (start us, length us, event | category | flops | bytes accessed | tf_op | source)
XLA Modules:
  0.0 180.6 jit_solution(7926887098573220511)
XLA Ops:
  7.2 1.5 constant_dynamic-slice_fusion.4
  9.4 1.7 bitcast_multiply_fusion.3
  11.1 3.0 %collective-permute-start = (bf16[1,8,128,128]{3,2,1,0:T(8,128)(2,1)}, bf16[1,8,128,128]{3,2,1,0:T(8,128)(2,1)}, u32[]{:S(2)}, u32[]{:S(2)}) collective-permute-start(bf16[1,8,128,128]{3,2,1,0:T(8,128)(2,1)} %bitcast_multiply_fusion.3), channel_id=1, source_target_pairs={{0,8},{8,16},{16,24},{24,0},{1,9},{9,17},{17,25},{25,1},{2,10},{10... | collective-permute-start | bytes 786440 | tf_op jit(solution)/shard_map/ppermute | solution.py:13
  14.1 2.0 %collective-permute-start.1 = (bf16[1,8,128,128]{3,2,1,0:T(8,128)(2,1)}, bf16[1,8,128,128]{3,2,1,0:T(8,128)(2,1)}, u32[]{:S(2)}, u32[]{:S(2)}) collective-permute-start(bf16[1,8,128,128]{3,2,1,0:T(8,128)(2,1)} %bitcast_multiply_fusion.3), channel_id=1, source_target_pairs={{0,24},{8,0},{16,8},{24,16},{1,25},{9,1},{17,9},{25,17},{2,26},{10... | collective-permute-start | bytes 786440 | tf_op jit(solution)/shard_map/ppermute | solution.py:16
  16.2 1.0 bitcast_multiply_fusion.4
  19.4 1.9 %fusion.78 = (bf16[1,1,128,4,128]{4,3,2,1,0:T(4,128)(2,1)S(1)}, bf16[1,1,128,4,128]{4,3,2,1,0:T(4,128)(2,1)}, bf16[1,1,128,4,128]{4,3,2,1,0:T(4,128)(2,1)}) fusion(bf16[3,1,128,4,128]{4,3,2,1,0:T(4,128)(2,1)} %param.8), kind=kLoop, calls=%fused_computation.113 | loop fusion | bytes 786432 | tf_op jit(solution)/shard_map/slice | solution.py:55
  23.2 1.2 fusion.65
  24.5 2.8 %fusion.45 = (bf16[512,4,128,1]{2,1,0,3:T(4,128)(2,1)S(1)}, bf16[512,4,128,1]{2,1,0,3:T(4,128)(2,1)S(1)}, bf16[512,4,128,1]{2,1,0,3:T(4,128)(2,1)S(1)}) fusion(bf16[3,1,512,4,128]{4,3,2,1,0:T(4,128)(2,1)S(1)} %copy-done, bf16[512]{0:T(512)(128)(2,1)S(1)} %get-tuple-element.26, bf16[4,128]{1,0:T(4,128)(2,1)S(1)} %get-tuple-element.20, ...), kind=kLoop, calls=%fused_computation.40 | loop fusion | flops 1572864 | bytes 3151872 | tf_op jit(solution)/shard_map/mul | solution.py:40
  28.4 1.2 copy_dynamic-update-slice_fusion.10
  29.6 1.1 copy_dynamic-update-slice_fusion.9
  30.8 7.4 %collective-permute-done.2 = bf16[1,8,128,128]{3,2,1,0:T(8,128)(2,1)S(1)} collective-permute-done((bf16[1,8,128,128]{3,2,1,0:T(8,128)(2,1)}, bf16[1,8,128,128]{3,2,1,0:T(8,128)(2,1)S(1)}, u32[]{:S(2)}, u32[]{:S(2)}) %collective-permute-start.2) | collective-permute-done | bytes 262176 | tf_op jit(solution)/shard_map/ppermute | solution.py:13
  38.4 5.6 %convert_bitcast_fusion.2 = bf16[8,4,512,128]{3,0,1,2:T(8,128)(2,1)} fusion(bf16[8,512,128]{2,0,1:T(8,128)(2,1)S(1)} %copy_dynamic-update-slice_fusion.8, f32[3,4,8,8]{3,2,1,0:T(8,128)} %param.9), kind=kOutput, calls=%fused_computation.11 | convolution fusion | flops 203423744 | bytes 5259264 | tf_op jit(solution)/shard_map/sdc,bcik->bdsik/dot_general | solution.py:42
  44.0 4.4 %fusion.15 = bf16[8,4,128,128]{3,2,0,1:T(8,128)(2,1)S(1)} fusion(bf16[8,4,512,128]{3,0,1,2:T(8,128)(2,1)} %convert_bitcast_fusion.2, bf16[512,4,128,1]{2,1,0,3:T(4,128)(2,1)S(1)} %get-tuple-element.3, bf16[1,1,128,4,128]{4,3,2,1,0:T(4,128)(2,1)S(1)} %copy-done.2), kind=kOutput, calls=%fused_computation.21 | convolution fusion | flops 672137216 | bytes 5898240 | tf_op jit(solution)/shard_map/bdsok,ksl->bdsol/dot_general | solution.py:52
  48.4 0.9 fusion.16
  49.6 17.1 %all_to_all.15 = bf16[4,1,8,128,128]{4,3,2,1,0:T(8,128)(2,1)S(1)} all-to-all(bf16[4,1,8,128,128]{4,3,2,1,0:T(8,128)(2,1)S(1)} %copy.71), channel_id=1, replica_groups=mesh['section'=4,'sector'=4,'comp'=2] {'sector'}, dimensions={0} | all-to-all | bytes 2097152 | tf_op jit(solution)/shard_map/all_to_all | solution.py:64
  66.9 3.8 %collective-permute-start.4 = (bf16[1,8,128,128]{3,2,1,0:T(8,128)(2,1)S(1)}, bf16[1,8,128,128]{3,2,1,0:T(8,128)(2,1)S(1)}, u32[]{:S(2)}, u32[]{:S(2)}) collective-permute-start(bf16[1,8,128,128]{3,2,1,0:T(8,128)(2,1)S(1)} %bitcast.208), channel_id=1, source_target_pairs={{0,24},{8,0},{16,8},{24,16},{1,25},{9,1},{17,9},{25,17},{2,26},{10... | collective-permute-start | bytes 786440 | tf_op jit(solution)/shard_map/ppermute | solution.py:16
  71.1 6.9 %collective-permute-done.3 = bf16[1,8,128,128]{3,2,1,0:T(8,128)(2,1)S(1)} collective-permute-done((bf16[1,8,128,128]{3,2,1,0:T(8,128)(2,1)S(1)}, bf16[1,8,128,128]{3,2,1,0:T(8,128)(2,1)S(1)}, u32[]{:S(2)}, u32[]{:S(2)}) %collective-permute-start.3) | collective-permute-done | bytes 262176 | tf_op jit(solution)/shard_map/ppermute | solution.py:13
  78.2 2.1 %collective-permute-done.4 = bf16[1,8,128,128]{3,2,1,0:T(8,128)(2,1)S(1)} collective-permute-done((bf16[1,8,128,128]{3,2,1,0:T(8,128)(2,1)S(1)}, bf16[1,8,128,128]{3,2,1,0:T(8,128)(2,1)S(1)}, u32[]{:S(2)}, u32[]{:S(2)}) %collective-permute-start.4) | collective-permute-done | bytes 262176 | tf_op jit(solution)/shard_map/ppermute | solution.py:16
  80.5 7.2 %collective-permute-done.5 = bf16[1,8,128,128]{3,2,1,0:T(8,128)(2,1)S(1)} collective-permute-done((bf16[1,8,128,128]{3,2,1,0:T(8,128)(2,1)S(1)}, bf16[1,8,128,128]{3,2,1,0:T(8,128)(2,1)S(1)}, u32[]{:S(2)}, u32[]{:S(2)}) %collective-permute-start.5) | collective-permute-done | bytes 262176 | tf_op jit(solution)/shard_map/ppermute | solution.py:13
  87.9 4.9 %convert_bitcast_fusion.1 = bf16[8,4,512,128]{3,0,1,2:T(8,128)(2,1)} fusion(bf16[8,512,128]{2,0,1:T(8,128)(2,1)S(1)} %copy_dynamic-update-slice_fusion.4, f32[3,4,8,8]{3,2,1,0:T(8,128)S(1)} %copy-done.3), kind=kOutput, calls=%fused_computation.10 | convolution fusion | flops 203423744 | bytes 5259264 | tf_op jit(solution)/shard_map/sdc,bcik->bdsik/dot_general | solution.py:42
  92.8 4.4 %fusion.17 = bf16[8,4,128,128]{3,2,0,1:T(8,128)(2,1)S(1)} fusion(bf16[8,4,512,128]{3,0,1,2:T(8,128)(2,1)} %convert_bitcast_fusion.1, bf16[512,4,128,1]{2,1,0,3:T(4,128)(2,1)S(1)} %get-tuple-element.4, bf16[1,1,128,4,128]{4,3,2,1,0:T(4,128)(2,1)S(1)} %copy-done.1), kind=kOutput, calls=%fused_computation.23 | convolution fusion | flops 672137216 | bytes 5898240 | tf_op jit(solution)/shard_map/bdsok,ksl->bdsol/dot_general | solution.py:52
  98.4 16.9 %all_to_all.16 = bf16[4,1,8,128,128]{4,3,2,1,0:T(8,128)(2,1)S(1)} all-to-all(bf16[4,1,8,128,128]{4,3,2,1,0:T(8,128)(2,1)S(1)} %copy.81), channel_id=1, replica_groups=mesh['section'=4,'sector'=4,'comp'=2] {'sector'}, dimensions={0} | all-to-all | bytes 2097152 | tf_op jit(solution)/shard_map/all_to_all | solution.py:64
  115.5 3.8 %collective-permute-start.7 = (bf16[1,8,128,128]{3,2,1,0:T(8,128)(2,1)S(1)}, bf16[1,8,128,128]{3,2,1,0:T(8,128)(2,1)S(1)}, u32[]{:S(2)}, u32[]{:S(2)}) collective-permute-start(bf16[1,8,128,128]{3,2,1,0:T(8,128)(2,1)S(1)} %bitcast.211), channel_id=1, source_target_pairs={{0,24},{8,0},{16,8},{24,16},{1,25},{9,1},{17,9},{25,17},{2,26},{10... | collective-permute-start | bytes 786440 | tf_op jit(solution)/shard_map/ppermute | solution.py:16
  119.7 6.9 %collective-permute-done.6 = bf16[1,8,128,128]{3,2,1,0:T(8,128)(2,1)S(1)} collective-permute-done((bf16[1,8,128,128]{3,2,1,0:T(8,128)(2,1)S(1)}, bf16[1,8,128,128]{3,2,1,0:T(8,128)(2,1)S(1)}, u32[]{:S(2)}, u32[]{:S(2)}) %collective-permute-start.6) | collective-permute-done | bytes 262176 | tf_op jit(solution)/shard_map/ppermute | solution.py:13
  126.7 2.1 %collective-permute-done.7 = bf16[1,8,128,128]{3,2,1,0:T(8,128)(2,1)S(1)} collective-permute-done((bf16[1,8,128,128]{3,2,1,0:T(8,128)(2,1)S(1)}, bf16[1,8,128,128]{3,2,1,0:T(8,128)(2,1)S(1)}, u32[]{:S(2)}, u32[]{:S(2)}) %collective-permute-start.7) | collective-permute-done | bytes 262176 | tf_op jit(solution)/shard_map/ppermute | solution.py:16
  129.1 7.2 %collective-permute-done.8 = bf16[1,8,128,128]{3,2,1,0:T(8,128)(2,1)S(1)} collective-permute-done((bf16[1,8,128,128]{3,2,1,0:T(8,128)(2,1)S(1)}, bf16[1,8,128,128]{3,2,1,0:T(8,128)(2,1)S(1)}, u32[]{:S(2)}, u32[]{:S(2)}) %collective-permute-start.8) | collective-permute-done | bytes 262176 | tf_op jit(solution)/shard_map/ppermute | solution.py:13
  136.4 4.9 %convert_bitcast_fusion = bf16[8,4,512,128]{3,0,1,2:T(8,128)(2,1)} fusion(bf16[8,512,128]{2,0,1:T(8,128)(2,1)S(1)} %copy_dynamic-update-slice_fusion, f32[3,4,8,8]{3,2,1,0:T(8,128)S(1)} %copy-done.3), kind=kOutput, calls=%fused_computation.9 | convolution fusion | flops 203423744 | bytes 5259264 | tf_op jit(solution)/shard_map/sdc,bcik->bdsik/dot_general | solution.py:42
  141.3 4.4 %fusion.19 = bf16[8,4,128,128]{3,2,0,1:T(8,128)(2,1)S(1)} fusion(bf16[8,4,512,128]{3,0,1,2:T(8,128)(2,1)} %convert_bitcast_fusion, bf16[512,4,128,1]{2,1,0,3:T(4,128)(2,1)S(1)} %get-tuple-element.2, bf16[1,1,128,4,128]{4,3,2,1,0:T(4,128)(2,1)S(1)} %get-tuple-element.5), kind=kOutput, calls=%fused_computation.25 | convolution fusion | flops 672137216 | bytes 5898240 | tf_op jit(solution)/shard_map/bdsok,ksl->bdsol/dot_general | solution.py:52
  146.9 16.9 %all_to_all.17 = bf16[4,1,8,128,128]{4,3,2,1,0:T(8,128)(2,1)S(1)} all-to-all(bf16[4,1,8,128,128]{4,3,2,1,0:T(8,128)(2,1)S(1)} %copy.91), channel_id=1, replica_groups=mesh['section'=4,'sector'=4,'comp'=2] {'sector'}, dimensions={0} | all-to-all | bytes 2097152 | tf_op jit(solution)/shard_map/all_to_all | solution.py:64
  163.8 0.9 reduce_sum.48
  164.7 1.9 %maximum_bitcast_fusion = bf16[3,1,8,1,128,128]{5,4,3,2,1,0:T(8,128)(2,1)} fusion(bf16[1,1,8,128,128]{4,3,2,1,0:T(8,128)(2,1)} %bitcast.213, bf16[1,1,8,128,128]{4,3,2,1,0:T(8,128)(2,1)S(1)} %bitcast.212, bf16[1,1,8,128,128]{4,3,2,1,0:T(8,128)(2,1)S(1)} %bitcast.209), kind=kLoop, calls=%fused_computation.36 | loop fusion | flops 786432 | bytes 1572864 | tf_op jit(solution)/shard_map/broadcast_in_dim | solution.py:68
  166.7 7.1 %reduce-scatter.2.cloned.1.call-done = bf16[4,128,128]{2,1,0:T(8,128)(2,1)} async-done(((bf16[8,128,128]{2,1,0:T(8,128)(2,1)}), bf16[4,128,128]{2,1,0:T(8,128)(2,1)}) %reduce-scatter.2.cloned.1.call-update) | async-done | bytes 131088 | tf_op jit(solution)/shard_map/reduce_scatter | solution.py:70
  (49 shorter events, 11.0 us)
Async XLA Ops:
  7.2 17.3 %copy-start = (bf16[3,1,512,4,128]{4,3,2,1,0:T(4,128)(2,1)S(1)}, bf16[3,1,512,4,128]{4,3,2,1,0:T(4,128)(2,1)}, u32[]{:S(2)}) copy-start(bf16[3,1,512,4,128]{4,3,2,1,0:T(4,128)(2,1)} %param.7) | copy-start | bytes 4718596
  7.2 166.6 %reduce-scatter.2.cloned.1.call-start = ((), (), s32[]{:S(2)}) async-start(), calls=%async_computation.4 | async-start | bytes 393216 | tf_op jit(solution)/shard_map/reduce_scatter | solution.py:70
  11.1 17.3 %collective-permute-start = (bf16[1,8,128,128]{3,2,1,0:T(8,128)(2,1)}, bf16[1,8,128,128]{3,2,1,0:T(8,128)(2,1)}, u32[]{:S(2)}, u32[]{:S(2)}) collective-permute-start(bf16[1,8,128,128]{3,2,1,0:T(8,128)(2,1)} %bitcast_multiply_fusion.3), channel_id=1, source_target_pairs={{0,8},{8,16},{16,24},{24,0},{1,9},{9,17},{17,25},{25,1},{2,10},{10... | collective-permute-start | bytes 786440 | tf_op jit(solution)/shard_map/ppermute | solution.py:13
  14.1 15.5 %collective-permute-start.1 = (bf16[1,8,128,128]{3,2,1,0:T(8,128)(2,1)}, bf16[1,8,128,128]{3,2,1,0:T(8,128)(2,1)}, u32[]{:S(2)}, u32[]{:S(2)}) collective-permute-start(bf16[1,8,128,128]{3,2,1,0:T(8,128)(2,1)} %bitcast_multiply_fusion.3), channel_id=1, source_target_pairs={{0,24},{8,0},{16,8},{24,16},{1,25},{9,1},{17,9},{25,17},{2,26},{10... | collective-permute-start | bytes 786440 | tf_op jit(solution)/shard_map/ppermute | solution.py:16
  27.3 16.7 %copy-start.2 = (bf16[1,1,128,4,128]{4,3,2,1,0:T(4,128)(2,1)S(1)}, bf16[1,1,128,4,128]{4,3,2,1,0:T(4,128)(2,1)}, u32[]{:S(2)}) copy-start(bf16[1,1,128,4,128]{4,3,2,1,0:T(4,128)(2,1)} %get-tuple-element.7) | copy-start | bytes 393220
  28.4 9.8 %collective-permute-start.2 = (bf16[1,8,128,128]{3,2,1,0:T(8,128)(2,1)}, bf16[1,8,128,128]{3,2,1,0:T(8,128)(2,1)S(1)}, u32[]{:S(2)}, u32[]{:S(2)}) collective-permute-start(bf16[1,8,128,128]{3,2,1,0:T(8,128)(2,1)} %collective-permute-done), channel_id=1, source_target_pairs={{0,8},{8,16},{16,24},{24,0},{1,9},{9,17},{17,25},{25,1},{2,10},{10... | collective-permute-start | bytes 786440 | tf_op jit(solution)/shard_map/ppermute | solution.py:13
  49.3 38.5 %copy-start.3 = (f32[3,4,8,8]{3,2,1,0:T(8,128)S(1)}, f32[3,4,8,8]{3,2,1,0:T(8,128)}, u32[]{:S(2)}) copy-start(f32[3,4,8,8]{3,2,1,0:T(8,128)} %param.9) | copy-start | bytes 9220
  66.9 25.9 %copy-start.1 = (bf16[1,1,128,4,128]{4,3,2,1,0:T(4,128)(2,1)S(1)}, bf16[1,1,128,4,128]{4,3,2,1,0:T(4,128)(2,1)}, u32[]{:S(2)}) copy-start(bf16[1,1,128,4,128]{4,3,2,1,0:T(4,128)(2,1)} %get-tuple-element.6) | copy-start | bytes 393220
  66.9 11.1 %collective-permute-start.3 = (bf16[1,8,128,128]{3,2,1,0:T(8,128)(2,1)S(1)}, bf16[1,8,128,128]{3,2,1,0:T(8,128)(2,1)S(1)}, u32[]{:S(2)}, u32[]{:S(2)}) collective-permute-start(bf16[1,8,128,128]{3,2,1,0:T(8,128)(2,1)S(1)} %bitcast.207), channel_id=1, source_target_pairs={{0,8},{8,16},{16,24},{24,0},{1,9},{9,17},{17,25},{25,1},{2,10},{10... | collective-permute-start | bytes 786440 | tf_op jit(solution)/shard_map/ppermute | solution.py:13
  66.9 13.4 %collective-permute-start.4 = (bf16[1,8,128,128]{3,2,1,0:T(8,128)(2,1)S(1)}, bf16[1,8,128,128]{3,2,1,0:T(8,128)(2,1)S(1)}, u32[]{:S(2)}, u32[]{:S(2)}) collective-permute-start(bf16[1,8,128,128]{3,2,1,0:T(8,128)(2,1)S(1)} %bitcast.208), channel_id=1, source_target_pairs={{0,24},{8,0},{16,8},{24,16},{1,25},{9,1},{17,9},{25,17},{2,26},{10... | collective-permute-start | bytes 786440 | tf_op jit(solution)/shard_map/ppermute | solution.py:16
  78.0 9.7 %collective-permute-start.5 = (bf16[1,8,128,128]{3,2,1,0:T(8,128)(2,1)S(1)}, bf16[1,8,128,128]{3,2,1,0:T(8,128)(2,1)S(1)}, u32[]{:S(2)}, u32[]{:S(2)}) collective-permute-start(bf16[1,8,128,128]{3,2,1,0:T(8,128)(2,1)S(1)} %collective-permute-done.3), channel_id=1, source_target_pairs={{0,8},{8,16},{16,24},{24,0},{1,9},{9,17},{17,25},{25,1},{2,10},{10... | collective-permute-start | bytes 786440 | tf_op jit(solution)/shard_map/ppermute | solution.py:13
  115.4 11.1 %collective-permute-start.6 = (bf16[1,8,128,128]{3,2,1,0:T(8,128)(2,1)S(1)}, bf16[1,8,128,128]{3,2,1,0:T(8,128)(2,1)S(1)}, u32[]{:S(2)}, u32[]{:S(2)}) collective-permute-start(bf16[1,8,128,128]{3,2,1,0:T(8,128)(2,1)S(1)} %bitcast.210), channel_id=1, source_target_pairs={{0,8},{8,16},{16,24},{24,0},{1,9},{9,17},{17,25},{25,1},{2,10},{10... | collective-permute-start | bytes 786440 | tf_op jit(solution)/shard_map/ppermute | solution.py:13
  115.5 13.4 %collective-permute-start.7 = (bf16[1,8,128,128]{3,2,1,0:T(8,128)(2,1)S(1)}, bf16[1,8,128,128]{3,2,1,0:T(8,128)(2,1)S(1)}, u32[]{:S(2)}, u32[]{:S(2)}) collective-permute-start(bf16[1,8,128,128]{3,2,1,0:T(8,128)(2,1)S(1)} %bitcast.211), channel_id=1, source_target_pairs={{0,24},{8,0},{16,8},{24,16},{1,25},{9,1},{17,9},{25,17},{2,26},{10... | collective-permute-start | bytes 786440 | tf_op jit(solution)/shard_map/ppermute | solution.py:16
  126.5 9.7 %collective-permute-start.8 = (bf16[1,8,128,128]{3,2,1,0:T(8,128)(2,1)S(1)}, bf16[1,8,128,128]{3,2,1,0:T(8,128)(2,1)S(1)}, u32[]{:S(2)}, u32[]{:S(2)}) collective-permute-start(bf16[1,8,128,128]{3,2,1,0:T(8,128)(2,1)S(1)} %collective-permute-done.6), channel_id=1, source_target_pairs={{0,8},{8,16},{16,24},{24,0},{1,9},{9,17},{17,25},{25,1},{2,10},{10... | collective-permute-start | bytes 786440 | tf_op jit(solution)/shard_map/ppermute | solution.py:13
Sparse Core Ops, SparseCore 0:
  164.9 8.8 reduce-scatter.1
